TPU v7x, 128 devices: a whole 4x4x4 slice. The times are simulated.
128 devices in a mesh: row: 8 (over x, core), col: 4 (over z), depth: 4 (over y).
Axes of the slice: x: 4, y: 4, z: 4, core: 2. Of those that a mesh axis runs over, the one named last changes fastest.
Arguments:
- packed: bfloat16 [36864, 2304], P(('row', 'col', 'depth')), may hold values from -6 to 6
- slot_blocks: int32 [36864], replicated, may hold values from 0 to 36863, as said below
- flip_bits: int32 [36864], P(('row', 'col', 'depth')), may hold values 0 or 1
- ladder_v: bfloat16 [36, 2304, 2048], P('depth', None, 'col'), may hold values from -0.01953125 to 0.01953125
Outputs:
- ladder: float32 [1024, 2048], P(('row', 'depth'), 'col')
Inputs may be any that keep to these rules, and one draw needn't show every extreme that they name: `slot_blocks`: every block id appears exactly once. The device at mesh position (r, c, e) in row, col, depth order holds slots k from (r * col count + c) * depth count + e times 288 onward; it holds only blocks whose pair p has p mod col count equal to c, and exactly 9 blocks for each pair of indices (p // 128, t // 9).
All inputs are finite; a program needn't handle non-finite values. No bound on the sum of `flip_bits` on one device may be relied on, other than what follows from the above.
Results may differ from a plain program's by a relative error of at most 0.0003.
Values may be sent and summed in bfloat16 or wider, within the bound.
A program may use at most 192 MiB of HBM per device.

v0:
```python
import jax
import jax.numpy as jnp
import numpy as np
from jax import lax
from jax.sharding import PartitionSpec as P

NV = 384
NB = 8


def tile_weights(blocks):
    values = [
        0.5 if first == second else 1.0
        for first in range(blocks)
        for second in range(first, blocks)
    ]
    return jnp.asarray(np.array(values, dtype=np.float32))


def unpack(packed, flip_bits, tile_side):
    count = packed.shape[0]
    tiles = packed.reshape(count, tile_side, tile_side)
    turned = -jnp.swapaxes(tiles, 1, 2)
    chosen = jnp.where((flip_bits == 1)[:, None, None], turned, tiles)
    return chosen.reshape(count, tile_side * tile_side)


def per_device(packed, slot_blocks, flip_bits, ladder_v):
    n_row = lax.axis_size("row")
    n_col = lax.axis_size("col")
    n_depth = lax.axis_size("depth")
    devices = n_row * n_col * n_depth
    slots, tile_len = packed.shape
    tiles_per = ladder_v.shape[0]
    cols_here = ladder_v.shape[2]
    tile_count = NB * (NB + 1) // 2
    tile_side = NV // NB
    pair_rows = slots * devices // tile_count // n_row
    groups = n_row * n_depth
    per_peer = slots // groups
    col_rows = pair_rows // n_col
    my_row = lax.axis_index("row")
    my_col = lax.axis_index("col")
    my_depth = lax.axis_index("depth")
    all_ids = slot_blocks.reshape(devices, slots)
    all_group = all_ids // tile_count // pair_rows * n_depth + all_ids % tile_count // tiles_per
    own_flat = (my_row * n_col + my_col) * n_depth + my_depth
    own_group = lax.dynamic_index_in_dim(all_group, own_flat, 0, keepdims=False)
    send_order = jnp.argsort(own_group, stable=True)
    canonical = unpack(packed, flip_bits, tile_side)
    outgoing = jnp.take(canonical, send_order, axis=0)
    matches = all_group == my_row * n_depth + my_depth
    hit_rank = jnp.cumsum(matches.astype(jnp.int32), 1) - 1
    incoming_ids = (
        jnp.zeros((devices, per_peer), jnp.int32)
        .at[jnp.arange(devices)[:, None], jnp.where(matches, hit_rank, per_peer)]
        .set(all_ids, mode="drop")
    )
    local_pair = incoming_ids // tile_count % pair_rows
    local_tile = incoming_ids % tile_count % tiles_per
    weights = lax.dynamic_slice_in_dim(tile_weights(NB), my_depth * tiles_per, tiles_per).astype(
        ladder_v.dtype
    )
    scaled_v = (ladder_v * weights[:, None, None]).reshape(tiles_per * tile_len, cols_here)
    copies = jnp.broadcast_to(
        outgoing.reshape(n_row, 1, n_depth, per_peer, tile_len),
        (n_row, n_col, n_depth, per_peer, tile_len),
    ).reshape(devices, per_peer, tile_len)
    arrived = lax.all_to_all(
        copies, ("row", "col", "depth"), split_axis=0, concat_axis=0, tiled=True
    )
    target = (
        (local_pair % n_col * col_rows + local_pair // n_col) * tiles_per + local_tile
    ).reshape(-1)
    place_order = jnp.argsort(target, stable=True)
    dense = jnp.take(arrived.reshape(-1, tile_len), place_order, axis=0)
    dense = dense.reshape(pair_rows, tiles_per * tile_len)
    partial_value = jnp.dot(dense, scaled_v, preferred_element_type=jnp.float32)
    natural = (
        partial_value.reshape(n_col, col_rows, cols_here)
        .transpose(1, 0, 2)
        .reshape(pair_rows, cols_here)
    )
    return lax.psum_scatter(natural, "depth", scatter_dimension=0, tiled=True)


def solution(mesh):
    in_specs = (
        P(("row", "col", "depth"), None),
        P(),
        P(("row", "col", "depth")),
        P("depth", None, "col"),
    )
    out_specs = P(("row", "depth"), "col")
    return jax.shard_map(
        per_device, mesh=mesh, in_specs=in_specs, out_specs=out_specs, check_vma=False
    )
```

profile of v0, /device:TPU:4, one launch (start us, length us, event | category | flops | bytes accessed | tf_op | source)
XLA Modules:
  0.0 291.9 jit_solution(15408851005837683610)
XLA Ops:
  6.5 1.0 sign_compare_fusion
  7.5 1.0 broadcast_divide_fusion
  8.5 0.2 reshape.138
  8.6 0.1 copy.42
  8.8 0.1 reshape.136
  8.9 0.1 copy.43
  9.0 0.1 reshape.134
  9.1 0.1 copy.41
  9.2 0.3 broadcast_compare_fusion
  9.5 0.2 dynamic-slice_reduce_fusion
  9.8 3.8 %sort.35 = (s32[288]{0:T(512)}, s32[288]{0:T(512)S(1)}) sort(s32[288]{0:T(512)S(1)} %dynamic-slice_reduce_fusion, s32[288]{0:T(512)S(1)} %iota.12), dimensions={0}, to_apply=%region_4.5 | sort | flops 2592 | bytes 4608 | tf_op jit(solution)/shard_map/jit(argsort)/sort | solution.py:49
  13.5 0.7 broadcast_compare_fusion.1
  14.2 0.1 broadcast_in_dim.62
  14.4 2.7 copy.52
  17.0 2.5 bitcast_select_fusion
  19.5 0.9 copy.54
  20.4 3.1 %gather_fusion = bf16[288,2304]{1,0:T(8,128)(2,1)} fusion(bf16[288,2304]{1,0:T(8,128)(2,1)S(1)} %copy.54, s32[1024]{0:T(1024)S(1)} %pad_clamp_fusion.1), kind=kCustom, calls=%fused_computation | custom fusion | bytes 2655360 | tf_op jit(solution)/shard_map/jit(_take)/gather | solution.py:51
  23.5 1.6 gather.13
  25.2 0.3 broadcast_select_fusion.1
  25.5 4.8 %broadcast_in_dim.67 = bf16[8,4,4,9,2304]{4,3,2,1,0:T(8,128)(2,1)} broadcast(bf16[8,4,9,2304]{3,2,1,0:T(8,128)(2,1)S(1)} %broadcast_select_fusion.1), dimensions={0,2,3,4} | broadcast | bytes 6635520 | tf_op jit(solution)/shard_map/broadcast_in_dim | solution.py:65
  30.3 0.0 copy-start.1
  30.3 0.0 copy-start
  30.3 0.0 copy-start.2
  30.3 10.9 %all-to-all-start = ((bf16[128,9,2304]{2,1,0:T(8,128)(2,1)}), bf16[128,9,2304]{2,1,0:T(8,128)(2,1)}, u32[]{:S(2)}, u32[]{:S(2)}) async-start(bf16[128,9,2304]{2,1,0:T(8,128)(2,1)} %bitcast.51), calls=%async_computation | async-start | bytes 18874368 | tf_op jit(solution)/shard_map/all_to_all | solution.py:69
  41.2 0.0 reduce-scatter.2.cloned.1.call-start
  41.3 0.1 fusion
  41.5 0.1 broadcast_add_fusion
  41.6 0.0 copy-done.1
  41.6 0.1 multiply_reduce_fusion
  41.7 0.0 copy-done
  41.7 0.1 and_reduce_fusion
  41.9 0.1 copy.50
  42.0 0.2 reshape.123
  42.2 135.4 %scatter_custom_fusion = s32[1152]{0:T(1024)S(1)} fusion(s32[36864]{0:T(1024)S(1)} %reshape.123, s32[36864]{0:T(1024)} %param.6, s32[]{:T(128)} %constant.128.clone.1), kind=kCustom, calls=%fused_computation.74 | custom fusion | bytes 5120
  177.7 0.1 copy.51
  177.8 0.2 reshape.88
  178.0 5.0 %sort.34 = (s32[1152]{0:T(1024)}, s32[1152]{0:T(1024)S(1)}) sort(s32[1152]{0:T(1024)S(1)} %reshape.88, s32[1152]{0:T(1024)S(1)} %iota.11), dimensions={0}, to_apply=%region_3.4 | sort | flops 12672 | bytes 18432 | tf_op jit(solution)/shard_map/jit(argsort)/sort | solution.py:75
  183.1 0.2 broadcast_in_dim.60
  183.3 0.0 copy-done.2
  183.3 0.1 dynamic_slice.11
  183.4 17.7 %broadcast_multiply_fusion = bf16[9,2304,512]{2,1,0:T(8,128)(2,1)} fusion(bf16[9,2304,512]{2,1,0:T(8,128)(2,1)} %param.8, bf16[9]{0:T(256)(128)(2,1)S(1)} %dynamic_slice.11), kind=kLoop, calls=%fused_computation.3 | loop fusion | flops 10616832 | bytes 42467344 | tf_op jit(solution)/shard_map/mul | solution.py:64
  201.1 0.0 all-to-all-done
  201.1 9.1 %reshape.92 = bf16[1152,2304]{1,0:T(8,128)(2,1)} reshape(bf16[128,9,2304]{2,1,0:T(8,128)(2,1)} %all-to-all-done) | data formatting | bytes 10616832 | tf_op jit(solution)/shard_map/reshape | solution.py:76
  210.2 15.0 %gather_fusion.1 = bf16[1152,2304]{1,0:T(8,128)(2,1)} fusion(bf16[1152,2304]{1,0:T(8,128)(2,1)} %reshape.92, s32[2048]{0:T(1024)S(1)} %pad_clamp_fusion), kind=kCustom, calls=%fused_computation.1 | custom fusion | bytes 10621440 | tf_op jit(solution)/shard_map/jit(_take)/gather | solution.py:76
  225.2 8.6 %gather.15 = bf16[128,9,2304]{2,1,0:T(8,128)(2,1)} reshape(bf16[1152,2304]{1,0:T(8,128)(2,1)} %gather_fusion.1) | data formatting | bytes 10616832 | tf_op jit(solution)/shard_map/jit(_take)/gather | solution.py:76
  233.8 8.3 %broadcast_select_fusion = bf16[128,9,2304]{2,1,0:T(8,128)(2,1)} fusion(bf16[128,9,2304]{2,1,0:T(8,128)(2,1)} %gather.15, pred[128,9]{1,0:T(8,128)(4,1)S(1)} %broadcast_in_dim.60), kind=kLoop, calls=%fused_computation.4 | loop fusion | flops 2654208 | bytes 10617984 | tf_op jit(solution)/shard_map/jit(_take)/select_n | solution.py:76
  242.1 9.4 %select_n.114 = bf16[4,32,20736]{2,1,0:T(8,128)(2,1)} reshape(bf16[128,9,2304]{2,1,0:T(8,128)(2,1)} %broadcast_select_fusion) | data formatting | bytes 10616832 | tf_op jit(solution)/shard_map/jit(_take)/select_n | solution.py:76
  251.5 10.1 %convolution_bitcast_fusion = f32[32,4,512]{2,0,1:T(8,128)S(1)} fusion(bf16[4,32,20736]{2,1,0:T(8,128)(2,1)} %select_n.114, bf16[20736,512,1]{1,0,2:T(8,128)(2,1)} %bitcast.50), kind=kOutput, calls=%fused_computation.8 | convolution fusion | flops 2717908992 | bytes 26804224 | tf_op jit(solution)/shard_map/dot_general | solution.py:78
  261.6 0.2 copy.55
  261.8 0.8 reshape.94
  262.6 0.0 reduce-scatter.2.cloned.1.call-update
  262.6 22.4 %reduce-scatter.2.cloned.1.call-done = f32[32,512]{1,0:T(8,128)} async-done(((f32[128,512]{1,0:T(8,128)}), f32[32,512]{1,0:T(8,128)}) %reduce-scatter.2.cloned.1.call-update) | async-done | bytes 65552 | tf_op jit(solution)/shard_map/reduce_scatter | solution.py:84
  (16 shorter events, 0.2 us)
Async XLA Ops:
  30.3 11.3 %copy-start.1 = (s32[2]{0:T(128)S(1)}, s32[2]{0:T(128)}, u32[]{:S(2)}) copy-start(s32[2]{0:T(128)} %constant.156) | copy-start | bytes 28
  30.3 11.4 %copy-start = (s32[2]{0:T(128)S(1)}, s32[2]{0:T(128)}, u32[]{:S(2)}) copy-start(s32[2]{0:T(128)} %constant.159) | copy-start | bytes 28
  30.3 153.0 %copy-start.2 = (bf16[36]{0:T(256)(128)(2,1)S(1)}, bf16[36]{0:T(256)(128)(2,1)}, u32[]{:S(2)}) copy-start(bf16[36]{0:T(256)(128)(2,1)} %constant.231) | copy-start | bytes 220
  30.3 170.8 %all-to-all-start = ((bf16[128,9,2304]{2,1,0:T(8,128)(2,1)}), bf16[128,9,2304]{2,1,0:T(8,128)(2,1)}, u32[]{:S(2)}, u32[]{:S(2)}) async-start(bf16[128,9,2304]{2,1,0:T(8,128)(2,1)} %bitcast.51), calls=%async_computation | async-start | bytes 18874368 | tf_op jit(solution)/shard_map/all_to_all | solution.py:69
  41.2 243.8 %reduce-scatter.2.cloned.1.call-start = ((), (), s32[]{:S(2)}) async-start(), calls=%async_computation.2 | async-start | bytes 327680 | tf_op jit(solution)/shard_map/reduce_scatter | solution.py:84
Sparse Core Ops, SparseCore 0:
  262.8 22.2 reduce-scatter.1
where the time goes:
time: 293 us; the launch traced here: 292 us
  local copies, waits for them, and re-layouts  194 us (66%)
  other arithmetic  41.1 us (14%)
  waiting for transfers between devices  22.4 us (8%)
  between operations  13.7 us (5%)
  starting transfers between devices  10.9 us (4%)
  matrix products  10.1 us (3%)
    unnamed x10, local copies, waits for them, and re-layouts  138 us
    gather x2, local copies, waits for them, and re-layouts, per_device(): dense = jnp.take(arrived.reshape(-1, tile_len), place_order, axis=0)  23.6 us
    reduce_scatter x1, waiting for transfers between devices, per_device(): return lax.psum_scatter(natural, 'depth', scatter_dimension=0, tiled=True)  22.4 us
    mul x1, other arithmetic, per_device(): ladder_v * weights[:, None, None]  17.7 us
    all_to_all x1, starting transfers between devices, per_device(): lax.all_to_all(copies, ('row', 'col', 'depth'), split_axis=0, concat_axis...  10.9 us
    dot_general x1, matrix products, per_device(): partial_value = jnp.dot(dense, scaled_v, preferred_element_type=jnp.float32)  10.1 us
    select_n x1, local copies, waits for them, and re-layouts, per_device(): dense = jnp.take(arrived.reshape(-1, tile_len), place_order, axis=0)  9.41 us
    reshape x1, local copies, waits for them, and re-layouts, per_device(): dense = jnp.take(arrived.reshape(-1, tile_len), place_order, axis=0)  9.07 us
  transfers between devices with their start and end apart: 2, of which 1 were waited for; matrix products, arithmetic and copies ran while one was open for 55% of the time, Pallas kernels for 0%

commit v1 on v0

v1 whole, which is shorter than its diff:
```python
import jax
import jax.numpy as jnp
import numpy as np
from jax import lax
from jax.experimental import pallas as pl
from jax.experimental.pallas import tpu as pltpu
from jax.sharding import PartitionSpec as P

MESH = pl.DeviceIdType.MESH
SIDE = 48
TILE = SIDE * SIDE
HALF = TILE // 2
SLOTS = 288
X_ORDER = (0, 1, 3, 2)
DIAGONAL = (0, 8, 15, 21, 26, 30, 33, 35)
F32 = jnp.float32
BF16 = jnp.bfloat16


def turn_matrix():
    turn = np.zeros((TILE, TILE), np.float32)
    first, second = np.divmod(np.arange(TILE), SIDE)
    turn[second * SIDE + first, np.arange(TILE)] = -1.0
    return turn.astype(jnp.bfloat16)


def dot(a, b):
    return jnp.dot(a, b, preferred_element_type=F32)


def iota(shape, dim):
    return lax.broadcasted_iota(jnp.int32, shape, dim)


def split_ids(ids):
    pair = ((ids >> 2) * 7282) >> 16
    tile = ids - pair * 36
    part = (tile * 57) >> 9
    group = (pair >> 7) * 4 + part
    place = (tile - part * 9) * 32 + ((pair & 127) >> 2)
    return group, place


def kernel(
    packed_hbm, ids_ref, flip_ref, v_hbm, turn_hbm, out_ref,
    packed, turn, v, kept, turned, sbuf, rbuf, ybuf, dense, places, cbuf, yrec, mixed,
    load_sem, ssend, srecv, zsend, zrecv, fsend, frecv, ysend, yrecv,
):
    r, c, e = lax.axis_index("row"), lax.axis_index("col"), lax.axis_index("depth")
    x, k = r // 2, lax.rem(r, 2)
    here = k * 4 + e
    up, down = lax.rem(c + 1, 4), lax.rem(c + 3, 4)

    load_packed = pltpu.make_async_copy(packed_hbm, packed, load_sem.at[0])
    load_turn = pltpu.make_async_copy(turn_hbm, turn, load_sem.at[1])
    load_v = pltpu.make_async_copy(v_hbm, v, load_sem.at[2])
    load_packed.start()
    load_turn.start()

    barrier = pltpu.get_barrier_semaphore()
    for step in range(1, 32):
        other = lax.rem(r * 4 + e + step, 32)
        pl.semaphore_signal(
            barrier, inc=1, device_id=(other // 4, c, lax.rem(other, 4)), device_id_type=MESH
        )
    for z in (up, down):
        pl.semaphore_signal(barrier, inc=1, device_id=(r, z, e), device_id_type=MESH)

    before = jnp.where(iota((SLOTS, SLOTS), 0) < iota((SLOTS, SLOTS), 1), 1.0, 0.0).astype(BF16)
    flat = (r * 4 + c) * 4 + e
    group, _ = split_ids(ids_ref[pl.ds(flat, 1), :])
    member = jnp.where(iota((32, SLOTS), 0) == group, 1.0, 0.0)
    rank = jnp.sum(member * dot(member.astype(BF16), before), axis=0, keepdims=True)
    target = group * 16 + rank.astype(jnp.int32)
    flips = flip_ref[...] == 1

    load_packed.wait()
    load_turn.wait()

    def sort_stage(q):
        x_to = lax.rem(x + 4 - q, 4)
        hit = target - x_to * 128 == iota((128, SLOTS), 0)
        chosen = jnp.concatenate(
            [
                jnp.where(hit & jnp.logical_not(flips), 1.0, 0.0),
                jnp.where(hit & flips, 1.0, 0.0),
            ],
            axis=0,
        ).astype(BF16)

        def pick(n, _):
            cols = pl.ds(pl.multiple_of(n * 256, 256), 256)
            rows = dot(chosen, packed[:, cols])
            kept[:, cols] = rows[:128].astype(BF16)
            turned[:, cols] = rows[128:].astype(BF16)
            return 0

        lax.fori_loop(0, 9, pick, 0)

        def flip(n, _):
            cols = pl.ds(pl.multiple_of(n * 256, 256), 256)
            rows = dot(turned[...], turn[:, cols]) + kept[:, cols].astype(F32)
            sbuf[q, :, :, cols] = rows.astype(BF16).reshape(8, 16, 256)
            return 0

        lax.fori_loop(0, 9, flip, 0)

    def block_copy(q, step):
        x_to = lax.rem(x + 4 - q, 4)
        to = lax.rem(here + step, 8)
        return pltpu.make_async_remote_copy(
            src_ref=sbuf.at[q, to],
            dst_ref=rbuf.at[q, here],
            send_sem=ssend.at[q, step],
            recv_sem=srecv.at[q, step],
            device_id=(x_to * 2 + to // 4, c, lax.rem(to, 4)),
            device_id_type=MESH,
        )

    def steps(q):
        return range(1 if q == 0 else 0, 8)

    def send_stage(q):
        sort_stage(q)
        for step in steps(q):
            block_copy(q, step).start()
        if q == 0:
            rbuf[0, here] = sbuf[0, here]

    line, column = iota((144, 128), 0), iota((144, 128), 1)
    compact = []
    for h in range(2):
        inner = line - 72 * h
        wanted = (inner & 7) * 16 + (inner >> 3)
        hit = (inner >= 0) & (inner < 72) & (column == wanted)
        compact.append(jnp.where(hit, 1.0, 0.0).astype(BF16))

    def z_copy(q, j, direction):
        piece = 3 * q + j
        return pltpu.make_async_remote_copy(
            src_ref=ybuf.at[0, piece],
            dst_ref=ybuf.at[3 if direction == 0 else 1, piece],
            send_sem=zsend.at[direction, piece],
            recv_sem=zrecv.at[direction, piece],
            device_id=(r, up if direction == 0 else down, e),
            device_id_type=MESH,
        )

    def forward_copy(q, j):
        piece = 3 * q + j
        direction = (3 * X_ORDER.index(q) + j) % 2
        return pltpu.make_async_remote_copy(
            src_ref=ybuf.at[3 if direction == 0 else 1, piece],
            dst_ref=ybuf.at[2, piece],
            send_sem=fsend.at[piece],
            recv_sem=frecv.at[piece],
            device_id=(r, up if direction == 0 else down, e),
            device_id_type=MESH,
        )

    def gather_stage(q):
        for step in steps(q):
            block_copy(q, step).wait_recv()
        for n in range(3):
            low, high = n * 384, HALF + n * 384
            first = rbuf[q, :, :, low:low + 384].reshape(128, 384)
            second = rbuf[q, :, :, high:high + 384].reshape(128, 384)
            rows = dot(compact[0], first) + dot(compact[1], second)
            ybuf[0, 3 * q:3 * q + 3, :, low:low + 384] = rows.astype(BF16).reshape(3, 48, 384)
        for j in range(3):
            for direction in range(2):
                z_copy(q, j, direction).start()

    def forward_stage(q):
        for j in range(3):
            direction = (3 * X_ORDER.index(q) + j) % 2
            z_copy(q, j, direction).wait_recv()
            forward_copy(q, j).start()

    def find_places():
        groups, place = split_ids(ids_ref[...])
        mine = groups == r * 4 + e
        nth = dot(jnp.where(mine, 1.0, 0.0).astype(BF16), before)
        nth = jnp.where(mine, nth, -1.0)
        place = place.astype(F32)
        lanes = iota((128, 128), 1)
        table = jnp.full((128, 128), -1.0, F32)
        for n in range(9):
            found = jnp.sum(jnp.where(nth == n, place, 0.0), axis=1, keepdims=True)
            table = jnp.where(lanes == n, found, table)
        for x_at in range(4):
            for k_at in range(2):
                for c_at in range(4):
                    low = x_at * 32 + k_at * 16 + c_at * 4
                    places[c_at, x_at, k_at * 4:k_at * 4 + 4, :] = table[low:low + 4, :]

    scale_tile = iota((SLOTS, 1), 0) // 32 + e * 9
    diagonal = jnp.zeros((SLOTS, 1), jnp.bool_)
    for t in DIAGONAL:
        diagonal = diagonal | (scale_tile == t)
    scale = jnp.where(diagonal, 0.5, 1.0)

    def contract(slot):
        c_at = lax.rem(c + slot, 4)
        lines = []
        for q in range(4):
            one = places[c_at, lax.rem(x + q, 4)]
            half = [jnp.broadcast_to(one[:, n:n + 1], (8, 128)) for n in range(9)]
            lines += half + half
        wanted = jnp.concatenate(lines + [jnp.full((64, 128), -1.0, F32)], axis=0)
        wanted = jnp.transpose(wanted)[0:1, :576]
        hit = jnp.where(iota((SLOTS, 576), 0).astype(F32) == wanted, scale, 0.0)
        second = lax.rem(iota((1, 576), 1), 144) >= 72
        order = [
            jnp.where(second, 0.0, hit).astype(BF16),
            jnp.where(second, hit, 0.0).astype(BF16),
        ]
        for h in range(2):
            for n in range(3):
                rows = ybuf[slot, :, :, n * 384:(n + 1) * 384].reshape(576, 384)
                low = h * HALF + n * 384
                dense[:, low:low + 384] = dot(order[h], rows).astype(BF16)

        def add(t, total):
            rows = dense[pl.ds(pl.multiple_of(t * 32, 32), 32), :]
            return total + dot(rows, v[t])

        total = lax.fori_loop(0, 9, add, jnp.zeros((32, 512), F32))
        cbuf[c_at] = total.reshape(4, 8, 512)
        for step in range(1, 4):
            sum_copy(slot, step).start()

    def sum_copy(slot, step):
        c_at = lax.rem(c + slot, 4)
        to = lax.rem(e + step, 4)
        return pltpu.make_async_remote_copy(
            src_ref=cbuf.at[c_at, to],
            dst_ref=yrec.at[step - 1, c_at],
            send_sem=ysend.at[slot, step],
            recv_sem=yrecv.at[slot, step],
            device_id=(r, c, to),
            device_id_type=MESH,
        )

    pl.semaphore_wait(barrier, 33)
    send_stage(0)
    load_v.start()
    send_stage(1)
    gather_stage(0)
    send_stage(3)
    gather_stage(1)
    send_stage(2)
    forward_stage(0)
    find_places()
    gather_stage(3)
    forward_stage(1)
    gather_stage(2)
    load_v.wait()
    contract(0)
    forward_stage(3)
    forward_stage(2)
    for slot in (3, 1):
        direction = 0 if slot == 3 else 1
        for at, q in enumerate(X_ORDER):
            for j in range(3):
                if (3 * at + j) % 2 != direction:
                    z_copy(q, j, direction).wait_recv()
        contract(slot)
    for q in X_ORDER:
        for j in range(3):
            forward_copy(q, j).wait_recv()
    contract(2)

    for slot in range(4):
        for step in range(1, 4):
            sum_copy(slot, step).wait_recv()
    for c_at in range(4):
        total = cbuf[c_at, e]
        for step in range(1, 4):
            total = total + yrec[step - 1, c_at]
        for n in range(4):
            mixed[n, pl.ds(c_at, 8, stride=4), :] = total[:, n * 128:(n + 1) * 128]
    for n in range(4):
        out_ref[:, n * 128:(n + 1) * 128] = mixed[n]

    for q in range(4):
        for step in steps(q):
            block_copy(q, step).wait_send()
        for j in range(3):
            z_copy(q, j, 0).wait_send()
            z_copy(q, j, 1).wait_send()
            forward_copy(q, j).wait_send()
        for step in range(1, 4):
            sum_copy(q, step).wait_send()


def per_device(packed, slot_blocks, flip_bits, ladder_v):
    any_space = pl.BlockSpec(memory_space=pl.ANY)
    in_vmem = pl.BlockSpec(memory_space=pltpu.VMEM)
    dma = pltpu.SemaphoreType.DMA
    return pl.pallas_call(
        kernel,
        out_shape=jax.ShapeDtypeStruct((32, 512), F32),
        in_specs=[any_space, in_vmem, in_vmem, any_space, any_space],
        out_specs=in_vmem,
        scratch_shapes=[
            pltpu.VMEM((SLOTS, TILE), BF16),
            pltpu.VMEM((TILE, TILE), BF16),
            pltpu.VMEM((9, TILE, 512), BF16),
            pltpu.VMEM((128, TILE), BF16),
            pltpu.VMEM((128, TILE), BF16),
            pltpu.VMEM((4, 8, 16, TILE), BF16),
            pltpu.VMEM((4, 8, 16, TILE), BF16),
            pltpu.VMEM((4, 12, 48, HALF), BF16),
            pltpu.VMEM((SLOTS, TILE), BF16),
            pltpu.VMEM((4, 4, 8, 128), F32),
            pltpu.VMEM((4, 4, 8, 512), F32),
            pltpu.VMEM((3, 4, 8, 512), F32),
            pltpu.VMEM((4, 32, 128), F32),
            dma((3,)),
            dma((4, 8)),
            dma((4, 8)),
            dma((2, 12)),
            dma((2, 12)),
            dma((12,)),
            dma((12,)),
            dma((4, 4)),
            dma((4, 4)),
        ],
        compiler_params=pltpu.CompilerParams(
            collective_id=0, has_side_effects=True, vmem_limit_bytes=62 * 2**20
        ),
    )(
        packed,
        slot_blocks.reshape(128, SLOTS),
        flip_bits.reshape(1, SLOTS),
        ladder_v,
        jnp.asarray(turn_matrix()),
    )


def solution(mesh):
    in_specs = (
        P(("row", "col", "depth"), None),
        P(),
        P(("row", "col", "depth")),
        P("depth", None, "col"),
    )
    out_specs = P(("row", "depth"), "col")
    return jax.shard_map(
        per_device, mesh=mesh, in_specs=in_specs, out_specs=out_specs, check_vma=False
    )
```

time: 293 us -> 104 us (0.35)
  local copies, waits for them, and re-layouts: 194 us -> 4.42 us
  Pallas kernels: 0 us -> 99.8 us
  other arithmetic: 41.1 us -> 0 us
  waiting for transfers between devices: 22.4 us -> 0 us
  between operations: 13.7 us -> 0.01 us
  starting transfers between devices: 10.9 us -> 0 us
  matrix products: 10.1 us -> 0 us
    unnamed x10 -> x1, local copies, waits for them, and re-layouts: 138 us -> 1.47 us
    pallas_call x0 -> x1, Pallas kernels: none -> 99.8 us  [per_device(): pl.pallas_call(kernel, out_shape=jax.ShapeDtypeStruct((32, 512), F32), in...]
    gather x4 -> x0, local copies, waits for them, and re-layouts: 28.3 us -> none  [the longest x2 23.6 us: per_device(): dense = jnp.take(arrived.reshape(-1, tile_len), place_order, axis=0)]
    reduce_scatter x1 -> x0, waiting for transfers between devices: 22.4 us -> none  [per_device(): return lax.psum_scatter(natural, 'depth', scatter_dimension=0, tiled=True)]
    mul x1 -> x0, other arithmetic: 17.7 us -> none  [per_device(): ladder_v * weights[:, None, None]]
    select_n x5 -> x0, other arithmetic: 11.1 us -> none  [the longest x2 8.29 us: per_device(): dense = jnp.take(arrived.reshape(-1, tile_len), place_order, axis=0)]
    all_to_all x1 -> x0, starting transfers between devices: 10.9 us -> none  [per_device(): lax.all_to_all(copies, ('row', 'col', 'depth'), split_axis=0, concat_axis...]
    dot_general x1 -> x0, matrix products: 10.1 us -> none  [per_device(): partial_value = jnp.dot(dense, scaled_v, preferred_element_type=jnp.float32)]
  transfers between devices with their start and end apart: 2 -> 0, of which waited for: 1 -> 0; matrix products, arithmetic and copies ran while one was open for 55% -> 0% of each run, Pallas kernels for 0% -> 0%
where the time goes in v1:
time: 104 us
  Pallas kernels  99.8 us (96%)
  local copies, waits for them, and re-layouts  4.42 us (4%)
    pallas_call x1, Pallas kernels, per_device(): pl.pallas_call(kernel, out_shape=jax.ShapeDtypeStruct((32, 512), F32), in...  99.8 us

profile of v1, /device:TPU:4, one launch (start us, length us, event | category | flops | bytes accessed | tf_op | source)
XLA Modules:
  0.0 104.2 jit_solution(11658495581353292599)
XLA Ops:
  0.0 1.2 %reshape.7.flip_ref = s32[1,288]{1,0:T(1,128)} reshape(s32[288]{0:T(512)} %param.7) | data formatting | bytes 2304 | tf_op jit(solution)/shard_map/reshape | solution.py:336
  1.2 1.7 %reshape.6.ids_ref = s32[128,288]{1,0:T(8,128)} reshape(s32[36864]{0:T(1024)} %param.6) | data formatting | bytes 294912 | tf_op jit(solution)/shard_map/reshape | solution.py:335
  2.9 99.8 %shard_map.55 = f32[32,512]{1,0:T(8,128)} custom-call(bf16[288,2304]{1,0:T(8,128)(2,1)} %packed_hbm.1, s32[128,288]{1,0:T(8,128)} %reshape.6.ids_ref, s32[1,288]{1,0:T(1,128)} %reshape.7.flip_ref, bf16[9,2304,512]{2,1,0:T(8,128)(2,1)} %v_hbm.1, bf16[2304,2304]{1,0:T(8,128)(2,1)} %constant.2.clone.turn_hbm), custom_call_target="tpu_custom_call" | custom-call | tf_op jit(solution)/shard_map/pallas_call | solution.py:301
  102.8 1.5 %copy.7 = f32[32,512]{1,0:T(8,128)} copy(f32[32,512]{1,0:T(8,128)} %shard_map.55) | data formatting | bytes 131072

commit v2 on v1

v2 whole, which is shorter than its diff:
```python
import jax
import jax.numpy as jnp
import numpy as np
from jax import lax
from jax.experimental import pallas as pl
from jax.experimental.pallas import tpu as pltpu
from jax.sharding import PartitionSpec as P


MESH = pl.DeviceIdType.MESH
TILE = 48 * 48
SLAB = 768
SLOTS = 288
X_ORDER = (0, 1, 3, 2)
DENSE_ORDER = (0, 3, 1, 2)
STEPS = ((0, 1), (0, 3), (1, 1), (1, 3), (0, 2), (1, 2), (1, 0))
DIAGONAL = (0, 8, 15, 21, 26, 30, 33, 35)
F32 = jnp.float32
BF16 = jnp.bfloat16


def part_matrix():
    a0, b1, b0 = np.meshgrid(np.arange(16), np.arange(3), np.arange(16), indexing="ij")
    out = np.zeros((SLAB, SLAB), np.float32)
    out[(a0 * 48 + b1 * 16 + b0).ravel(), (b1 * 256 + a0 * 16 + b0).ravel()] = 1.0
    return out.astype(jnp.bfloat16)


def dot(a, b):
    return jnp.dot(a, b, preferred_element_type=F32)


def iota(shape, dim):
    return lax.broadcasted_iota(jnp.int32, shape, dim)


def split_ids(ids):
    pair = ((ids >> 2) * 7282) >> 16
    tile = ids - pair * 36
    part = (tile * 57) >> 9
    group = (pair >> 7) * 4 + part
    place = (tile - part * 9) * 32 + ((pair & 127) >> 2)
    return group, place


def forward_direction(q, n):
    return (X_ORDER.index(q) + n) % 2


def kernel(
    packed_hbm, ids_hbm, flip_ref, v_hbm, part_hbm, out_ref,
    packed, ids_ref, part, v, nbuf, nrec, sbuf, xbuf, rbuf, ybuf, pmat, dense, table, places, cbuf, yrec, mixed,
    load_sem, v_sem, nsend, nrecv, xsend, xrecv, ssend, srecv, zsend, zrecv, fsend, frecv, ysend, yrecv,
):
    r, c, e = lax.axis_index("row"), lax.axis_index("col"), lax.axis_index("depth")
    x, k = r // 2, lax.rem(r, 2)
    here = k * 4 + e
    up, down = lax.rem(c + 1, 4), lax.rem(c + 3, 4)

    load_packed = pltpu.make_async_copy(packed_hbm, packed, load_sem.at[0])
    load_part = pltpu.make_async_copy(part_hbm, part, load_sem.at[1])
    load_ids = pltpu.make_async_copy(ids_hbm, ids_ref, load_sem.at[2])
    load_ids.start()
    load_packed.start()
    load_part.start()

    barrier = pltpu.get_barrier_semaphore()
    near = [(x * 2 + lax.rem(k + k_step, 2), c, lax.rem(e + e_step, 4)) for k_step, e_step in STEPS]
    near += [(lax.rem(x + step, 4) * 2 + k, c, e) for step in (1, 2, 3)]
    near += [(r, up, e), (r, down, e)]
    for device in near:
        pl.semaphore_signal(barrier, inc=1, device_id=device, device_id_type=MESH)

    def load_v(n, b):
        return pltpu.make_async_copy(v_hbm.at[:, n, :, b], v.at[n, :, b], v_sem.at[n, b])

    before = jnp.where(iota((SLOTS, SLOTS), 0) < iota((SLOTS, SLOTS), 1), 1.0, 0.0).astype(BF16)
    flat = (r * 4 + c) * 4 + e
    first = (flat * 9) // 4
    load_ids.wait()
    own = jnp.concatenate([ids_ref[pl.ds(first + i, 1), :] for i in range(3)], axis=1)
    own = pltpu.roll(own, lax.rem(384 - 32 * lax.rem(flat, 4), 384), 1)[:, :SLOTS]
    group, _ = split_ids(own)
    member = jnp.where(iota((32, SLOTS), 0) == group, 1.0, 0.0)
    rank = jnp.sum(member * dot(member.astype(BF16), before), axis=0, keepdims=True)
    target = group * 9 + rank.astype(jnp.int32)
    flips = flip_ref[...].reshape(1, SLOTS) == 1

    swap_in, swap_out = iota((256, 256), 0), iota((256, 256), 1)
    swap = (swap_in & 15) * 16 + (swap_in >> 4) == swap_out
    swap = jnp.where(swap, -1.0, 0.0).astype(BF16)

    def spread(a, rows):
        line, column = iota((8 * rows, 80), 0), iota((8 * rows, 80), 1)
        to, inner = line // rows, line % rows - 9 * a
        hit = (inner >= 0) & (inner < 9) & (column == to * 9 + inner)
        return jnp.where(hit, 1.0, 0.0).astype(BF16)

    spread_near = spread(0, 16)
    spread_far = [spread(a, 32) for a in range(3)]

    load_packed.wait()
    load_part.wait()

    def sort_stage(q):
        x_to = lax.rem(x + 4 - q, 4)
        line = iota((80, SLOTS), 0)
        hit = (target - x_to * 72 == line) & (line < 72)
        chosen = jnp.where(hit, 1.0, 0.0)
        turned = jnp.sum(jnp.where(flips, chosen, 0.0), axis=1, keepdims=True) > 0.5
        chosen = chosen.astype(BF16)
        parts = []
        for a in range(3):
            rows = dot(chosen, packed[:, a * SLAB:(a + 1) * SLAB]).astype(BF16)
            for b in range(3):
                parts.append(dot(rows, part[:, b * 256:(b + 1) * 256]))
        parts16 = [one.astype(BF16) for one in parts]

        def canon(a, b):
            return jnp.where(turned, dot(parts16[b * 3 + a], swap), parts[a * 3 + b]).astype(BF16)

        if q == 0:
            pl.semaphore_wait(barrier, len(near))
            for a in range(3):
                for b in range(3):
                    rows = dot(spread_near, canon(a, b)).astype(BF16)
                    nbuf[a, :, :, b * 256:(b + 1) * 256] = rows.reshape(8, 16, 256)
                send_near(a)
            return
        for b in range(3):
            total = dot(spread_far[0], canon(0, b))
            for a in range(1, 3):
                total = total + dot(spread_far[a], canon(a, b))
            sbuf[q - 1, :, :, b * 256:(b + 1) * 256] = total.astype(BF16).reshape(8, 32, 256)
        x_copy(q).start()

    def x_copy(q):
        return pltpu.make_async_remote_copy(
            src_ref=sbuf.at[q - 1],
            dst_ref=xbuf.at[q - 1],
            send_sem=xsend.at[q],
            recv_sem=xrecv.at[q],
            device_id=(lax.rem(x + 4 - q, 4) * 2 + k, c, e),
            device_id_type=MESH,
        )

    def near_place(step):
        k_step, e_step = STEPS[step]
        to_k, to_e = lax.rem(k + k_step, 2), lax.rem(e + e_step, 4)
        return to_k * 4 + to_e, (x * 2 + to_k, c, to_e)

    def near_copy(a, step):
        to, device = near_place(step)
        return pltpu.make_async_remote_copy(
            src_ref=nbuf.at[a, to],
            dst_ref=nrec.at[a, here],
            send_sem=nsend.at[a, step],
            recv_sem=nrecv.at[a, step],
            device_id=device,
            device_id_type=MESH,
        )

    def send_near(a):
        for step in range(7):
            near_copy(a, step).start()
        nrec[a, here] = nbuf[a, here]

    def block_copy(q, step):
        to, device = near_place(step)
        return pltpu.make_async_remote_copy(
            src_ref=xbuf.at[q - 1, to],
            dst_ref=rbuf.at[q - 1, here],
            send_sem=ssend.at[q, step],
            recv_sem=srecv.at[q, step],
            device_id=device,
            device_id_type=MESH,
        )

    def pass_blocks(q):
        x_copy(q).wait_recv()
        for step in range(7):
            block_copy(q, step).start()
        rbuf[q - 1, here] = xbuf[q - 1, here]

    def compact(n, h, rows):
        line, column = iota((144, 8 * rows), 0) - 72 * h, iota((144, 8 * rows), 1)
        wanted = (line & 7) * rows + n * 9 + (line >> 3)
        hit = (line >= 0) & (line < 72) & (column == wanted)
        return jnp.where(hit, 1.0, 0.0).astype(BF16)

    def z_copy(q, n, direction):
        at = X_ORDER.index(q)
        return pltpu.make_async_remote_copy(
            src_ref=ybuf.at[0, n, at],
            dst_ref=ybuf.at[3 if direction == 0 else 1, n, at],
            send_sem=zsend.at[direction, n, at],
            recv_sem=zrecv.at[direction, n, at],
            device_id=(r, up if direction == 0 else down, e),
            device_id_type=MESH,
        )

    def forward_copy(q, n):
        at = X_ORDER.index(q)
        direction = forward_direction(q, n)
        return pltpu.make_async_remote_copy(
            src_ref=ybuf.at[3 if direction == 0 else 1, n, at],
            dst_ref=ybuf.at[2, n, at],
            send_sem=fsend.at[n, at],
            recv_sem=frecv.at[n, at],
            device_id=(r, up if direction == 0 else down, e),
            device_id_type=MESH,
        )

    def send_piece(q, n, rows):
        ybuf[0, n, X_ORDER.index(q)] = rows.astype(BF16)
        for direction in range(2):
            z_copy(q, n, direction).start()

    def gather_near(n):
        for step in range(7):
            near_copy(n, step).wait_recv()
        low = nrec[n, :, :, :384].reshape(128, 384)
        high = nrec[n, :, :, 384:].reshape(128, 384)
        send_piece(0, n, dot(compact(0, 0, 16), low) + dot(compact(0, 1, 16), high))

    def gather_stage(q):
        for step in range(7):
            block_copy(q, step).wait_recv()
        low = rbuf[q - 1, :, :, :384].reshape(256, 384)
        high = rbuf[q - 1, :, :, 384:].reshape(256, 384)
        for n in range(3):
            send_piece(q, n, dot(compact(n, 0, 32), low) + dot(compact(n, 1, 32), high))

    def forward_stage(q, n):
        z_copy(q, n, forward_direction(q, n)).wait_recv()
        forward_copy(q, n).start()

    def wait_rest(slot, q, n):
        if slot == 2:
            forward_copy(q, n).wait_recv()
        elif slot != 0:
            direction = 0 if slot == 3 else 1
            if forward_direction(q, n) != direction:
                z_copy(q, n, direction).wait_recv()

    def find_places():
        ids = []
        for j in range(4):
            lines = [ids_ref[pl.ds((9 * j) // 4 + i, 32, stride=9), :] for i in range(3)]
            lines = jnp.concatenate(lines, axis=1)
            if j > 0:
                lines = pltpu.roll(lines, 384 - 32 * j, 1)
            ids.append(lines[:, :SLOTS])
        groups, place = split_ids(jnp.concatenate(ids, axis=0))
        mine = groups == r * 4 + e
        nth = dot(jnp.where(mine, 1.0, 0.0).astype(BF16), before)
        nth = jnp.where(mine, nth, -1.0)
        place = place.astype(F32)
        lanes = iota((128, 128), 1)
        found = jnp.full((128, 128), -1.0, F32)
        for n in range(9):
            value = jnp.sum(jnp.where(nth == n, place, 0.0), axis=1, keepdims=True)
            found = jnp.where(lanes == n, value, found)
        table[...] = found
        for j in range(4):
            for c_at in range(4):
                places[pl.ds(c_at * 32 + j, 8, stride=4), :] = table[pl.ds(j * 32 + c_at, 8, stride=4), :]

    scale_tile = iota((SLOTS, 1), 0) // 32 + e * 9
    diagonal = jnp.zeros((SLOTS, 1), jnp.bool_)
    for t in DIAGONAL:
        diagonal = diagonal | (scale_tile == t)
    scale = jnp.where(diagonal, 0.5, 1.0)

    none = jnp.full((8, 128), -1.0, F32)

    def find_order(slot):
        c_at = lax.rem(c + slot, 4)
        lines = [[], []]
        for q in X_ORDER:
            low = pl.multiple_of(c_at * 32 + lax.rem(x + q, 4) * 8, 8)
            one = places[pl.ds(low, 8), :]
            half = [jnp.broadcast_to(one[:, n:n + 1], (8, 128)) for n in range(9)]
            if q == X_ORDER[3]:
                lines = [line + [none, none] for line in lines]
            lines[0] += half + [none]
            lines[1] += [none] + half
        for h in range(2):
            wanted = jnp.transpose(jnp.concatenate(lines[h] + 6 * [none], axis=0))[0:1]
            hit = jnp.where(iota((SLOTS, 384), 0).astype(F32) == wanted, scale, 0.0)
            pmat[slot, h] = hit.astype(BF16)

    def place_blocks(slot, n, side):
        at = DENSE_ORDER.index(slot) * 32
        for h in range(2):
            if side == 0:
                blocks = [ybuf[slot, n, i, h * 64:h * 64 + 80, :] for i in range(3)]
                rows = dot(pmat[slot, h, :, :240], jnp.concatenate(blocks, axis=0))
            else:
                rows = dot(pmat[slot, h, :, 256:336], ybuf[slot, n, 3, h * 64:h * 64 + 80, :])
            rows = rows.reshape(9, 32, 384)
            cols = slice(h * 384, (h + 1) * 384)
            if side == 1:
                rows = rows + dense[n, :, at:at + 32, cols].astype(F32)
            dense[n, :, at:at + 32, cols] = rows.astype(BF16)

    def multiply(total, n, low, high):
        def add(t, total):
            return total + dot(dense[n, t, low:high, :], v[n, t].reshape(SLAB, 512))

        return lax.fori_loop(0, 9, add, total)

    def sum_copy(slot, step):
        c_at = lax.rem(c + slot, 4)
        to = lax.rem(e + step, 4)
        return pltpu.make_async_remote_copy(
            src_ref=cbuf.at[c_at, to],
            dst_ref=yrec.at[step - 1, c_at],
            send_sem=ysend.at[slot, step],
            recv_sem=yrecv.at[slot, step],
            device_id=(r, c, to),
            device_id_type=MESH,
        )

    def send_sums(slot, total):
        cbuf[lax.rem(c + slot, 4)] = total.reshape(4, 8, 512)
        for step in range(1, 4):
            sum_copy(slot, step).start()

    sort_stage(0)
    for n in range(3):
        for b in range(3):
            load_v(n, b).start()
    sort_stage(1)
    sort_stage(3)
    for n in range(3):
        gather_near(n)
    find_places()
    pass_blocks(1)
    sort_stage(2)
    for n in range(3):
        forward_stage(0, n)
    find_order(0)
    pass_blocks(3)
    gather_stage(1)
    for slot in (3, 1, 2):
        find_order(slot)
    gather_stage(3)
    for n in range(3):
        forward_stage(1, n)
    pass_blocks(2)
    for n in range(3):
        place_blocks(0, n, 0)
    gather_stage(2)
    for n in range(3):
        forward_stage(3, n)
    for n in range(3):
        for slot in (3, 1):
            for q in X_ORDER[:3]:
                wait_rest(slot, q, n)
            place_blocks(slot, n, 0)
        place_blocks(0, n, 1)
    for n in range(3):
        forward_stage(2, n)
    for n in range(3):
        for slot in (3, 1):
            wait_rest(slot, 2, n)
            place_blocks(slot, n, 1)
    total = jnp.zeros((96, 512), F32)
    for n in range(3):
        for b in range(3):
            load_v(n, b).wait()
        total = multiply(total, n, 0, 96)
    for at, slot in enumerate(DENSE_ORDER[:3]):
        send_sums(slot, total[at * 32:(at + 1) * 32])
    for n in range(3):
        for q in X_ORDER[:3]:
            wait_rest(2, q, n)
        place_blocks(2, n, 0)
    total = jnp.zeros((32, 512), F32)
    for n in range(3):
        wait_rest(2, 2, n)
        place_blocks(2, n, 1)
        total = multiply(total, n, 96, 128)
    send_sums(2, total)

    for slot in range(4):
        for step in range(1, 4):
            sum_copy(slot, step).wait_recv()
    for c_at in range(4):
        total = cbuf[c_at, e]
        for step in range(1, 4):
            total = total + yrec[step - 1, c_at]
        for n in range(4):
            mixed[n, pl.ds(c_at, 8, stride=4), :] = total[:, n * 128:(n + 1) * 128]
    for n in range(4):
        out_ref[:, n * 128:(n + 1) * 128] = mixed[n]

    for q in range(4):
        if q > 0:
            x_copy(q).wait_send()
            for step in range(7):
                block_copy(q, step).wait_send()
        else:
            for n in range(3):
                for step in range(7):
                    near_copy(n, step).wait_send()
        for n in range(3):
            z_copy(q, n, 0).wait_send()
            z_copy(q, n, 1).wait_send()
            forward_copy(q, n).wait_send()
        for step in range(1, 4):
            sum_copy(q, step).wait_send()


def per_device(packed, slot_blocks, flip_bits, ladder_v):
    any_space = pl.BlockSpec(memory_space=pl.ANY)
    in_vmem = pl.BlockSpec(memory_space=pltpu.VMEM)
    dma = pltpu.SemaphoreType.DMA
    return pl.pallas_call(
        kernel,
        out_shape=jax.ShapeDtypeStruct((32, 512), F32),
        in_specs=[any_space, any_space, in_vmem, any_space, any_space],
        out_specs=in_vmem,
        scratch_shapes=[
            pltpu.VMEM((SLOTS, TILE), BF16),
            pltpu.VMEM((SLOTS, 128), jnp.int32),
            pltpu.VMEM((SLAB, SLAB), BF16),
            pltpu.VMEM((3, 9, 3, 16, 16, 512), BF16),
            pltpu.VMEM((3, 8, 16, SLAB), BF16),
            pltpu.VMEM((3, 8, 16, SLAB), BF16),
            pltpu.VMEM((3, 8, 32, SLAB), BF16),
            pltpu.VMEM((3, 8, 32, SLAB), BF16),
            pltpu.VMEM((3, 8, 32, SLAB), BF16),
            pltpu.VMEM((4, 3, 4, 144, 384), BF16),
            pltpu.VMEM((4, 2, SLOTS, 384), BF16),
            pltpu.VMEM((3, 9, 128, SLAB), BF16),
            pltpu.VMEM((128, 128), F32),
            pltpu.VMEM((128, 128), F32),
            pltpu.VMEM((4, 4, 8, 512), F32),
            pltpu.VMEM((3, 4, 8, 512), F32),
            pltpu.VMEM((4, 32, 128), F32),
            dma((3,)),
            dma((3, 3)),
            dma((3, 7)),
            dma((3, 7)),
            dma((4,)),
            dma((4,)),
            dma((4, 7)),
            dma((4, 7)),
            dma((2, 3, 4)),
            dma((2, 3, 4)),
            dma((3, 4)),
            dma((3, 4)),
            dma((4, 4)),
            dma((4, 4)),
        ],
        compiler_params=pltpu.CompilerParams(
            collective_id=0, has_side_effects=True, vmem_limit_bytes=60 * 2**20
        ),
    )(
        packed,
        slot_blocks.reshape(SLOTS, 128),
        flip_bits,
        ladder_v.reshape(9, 3, 16, 3, 16, 512),
        jnp.asarray(part_matrix()),
    )


def solution(mesh):
    in_specs = (
        P(("row", "col", "depth"), None),
        P(),
        P(("row", "col", "depth")),
        P("depth", None, "col"),
    )
    out_specs = P(("row", "depth"), "col")
    return jax.shard_map(
        per_device, mesh=mesh, in_specs=in_specs, out_specs=out_specs, check_vma=False
    )
```

time: 104 us -> 80.7 us (0.78); the launches traced: 104 us -> 79.6 us
  Pallas kernels: 99.8 us -> 78.1 us
  local copies, waits for them, and re-layouts: 4.42 us -> 1.47 us
    pallas_call x1, Pallas kernels: 99.8 us -> 78.1 us  [per_device(): pl.pallas_call(kernel, out_shape=jax.ShapeDtypeStruct((32, 512), F32), in...]
    reshape x2 -> x0, local copies, waits for them, and re-layouts: 2.95 us -> none  [the longest x1 1.7 us: per_device(): slot_blocks.reshape(128, SLOTS)]
where the time goes in v2:
time: 80.7 us; the launch traced here: 79.6 us
  Pallas kernels  78.1 us (97%)
  local copies, waits for them, and re-layouts  1.47 us (2%)
    pallas_call x1, Pallas kernels, per_device(): pl.pallas_call(kernel, out_shape=jax.ShapeDtypeStruct((32, 512), F32), in...  78.1 us

profile of v2, /device:TPU:4, one launch (start us, length us, event | category | flops | bytes accessed | tf_op | source)
XLA Modules:
  0.0 79.6 jit_solution(10250228650023123770)
XLA Ops:
  0.0 78.1 %shard_map.55 = f32[32,512]{1,0:T(8,128)} custom-call(bf16[288,2304]{1,0:T(8,128)(2,1)} %packed_hbm.1, s32[288,128]{1,0:T(8,128)} %bitcast.3, s32[288]{0:T(512)} %flip_ref.1, bf16[9,3,16,3,16,512]{5,4,3,2,1,0:T(8,128)(2,1)} %bitcast.2, bf16[768,768]{1,0:T(8,128)(2,1)} %constant.2.clone.part_hbm), custom_call_target="tpu_custom_call" | custom-call | tf_op jit(solution)/shard_map/pallas_call | solution.py:420
  78.1 1.5 %copy.7 = f32[32,512]{1,0:T(8,128)} copy(f32[32,512]{1,0:T(8,128)} %shard_map.55) | data formatting | bytes 131072

commit v3 on v2

--- a/solution.py
+++ b/solution.py
@@ -12,7 +12,6 @@
 SLAB = 768
 SLOTS = 288
 X_ORDER = (0, 1, 3, 2)
-DENSE_ORDER = (0, 3, 1, 2)
 STEPS = ((0, 1), (0, 3), (1, 1), (1, 3), (0, 2), (1, 2), (1, 0))
 DIAGONAL = (0, 8, 15, 21, 26, 30, 33, 35)
 F32 = jnp.float32
@@ -43,13 +42,17 @@
     return group, place
 
 
-def forward_direction(q, n):
-    return (X_ORDER.index(q) + n) % 2
+def loop(count, body):
+    def step(i, carry):
+        body(i)
+        return carry
+
+    lax.fori_loop(0, count, step, 0)
 
 
 def kernel(
     packed_hbm, ids_hbm, flip_ref, v_hbm, part_hbm, out_ref,
-    packed, ids_ref, part, v, nbuf, nrec, sbuf, xbuf, rbuf, ybuf, pmat, dense, table, places, cbuf, yrec, mixed,
+    packed, ids_ref, part, v, nbuf, nrec, sbuf, xbuf, rbuf, ybuf, pmat, dense, late, total, near_lines, lines_of, table, places, cbuf, yrec, mixed,
     load_sem, v_sem, nsend, nrecv, xsend, xrecv, ssend, srecv, zsend, zrecv, fsend, frecv, ysend, yrecv,
 ):
     r, c, e = lax.axis_index("row"), lax.axis_index("col"), lax.axis_index("depth")
@@ -102,7 +105,7 @@
     load_packed.wait()
     load_part.wait()
 
-    def sort_stage(q):
+    def sort_stage(q, is_near):
         x_to = lax.rem(x + 4 - q, 4)
         line = iota((80, SLOTS), 0)
         hit = (target - x_to * 72 == line) & (line < 72)
@@ -119,20 +122,20 @@
         def canon(a, b):
             return jnp.where(turned, dot(parts16[b * 3 + a], swap), parts[a * 3 + b]).astype(BF16)
 
-        if q == 0:
+        if is_near:
             pl.semaphore_wait(barrier, len(near))
             for a in range(3):
                 for b in range(3):
                     rows = dot(spread_near, canon(a, b)).astype(BF16)
                     nbuf[a, :, :, b * 256:(b + 1) * 256] = rows.reshape(8, 16, 256)
-                send_near(a)
+                if a == 0:
+                    send_near(0)
             return
         for b in range(3):
             total = dot(spread_far[0], canon(0, b))
             for a in range(1, 3):
                 total = total + dot(spread_far[a], canon(a, b))
             sbuf[q - 1, :, :, b * 256:(b + 1) * 256] = total.astype(BF16).reshape(8, 32, 256)
-        x_copy(q).start()
 
     def x_copy(q):
         return pltpu.make_async_remote_copy(
@@ -188,60 +191,60 @@
         hit = (line >= 0) & (line < 72) & (column == wanted)
         return jnp.where(hit, 1.0, 0.0).astype(BF16)
 
-    def z_copy(q, n, direction):
-        at = X_ORDER.index(q)
+    def z_copy(at, n, direction):
         return pltpu.make_async_remote_copy(
             src_ref=ybuf.at[0, n, at],
-            dst_ref=ybuf.at[3 if direction == 0 else 1, n, at],
+            dst_ref=ybuf.at[3 - 2 * direction, n, at],
             send_sem=zsend.at[direction, n, at],
             recv_sem=zrecv.at[direction, n, at],
-            device_id=(r, up if direction == 0 else down, e),
+            device_id=(r, lax.rem(c + 1 + 2 * direction, 4), e),
             device_id_type=MESH,
         )
 
-    def forward_copy(q, n):
-        at = X_ORDER.index(q)
-        direction = forward_direction(q, n)
+    def forward_copy(at, n):
+        direction = lax.rem(at + n, 2)
         return pltpu.make_async_remote_copy(
-            src_ref=ybuf.at[3 if direction == 0 else 1, n, at],
+            src_ref=ybuf.at[3 - 2 * direction, n, at],
             dst_ref=ybuf.at[2, n, at],
             send_sem=fsend.at[n, at],
             recv_sem=frecv.at[n, at],
-            device_id=(r, up if direction == 0 else down, e),
+            device_id=(r, lax.rem(c + 1 + 2 * direction, 4), e),
             device_id_type=MESH,
         )
 
-    def send_piece(q, n, rows):
-        ybuf[0, n, X_ORDER.index(q)] = rows.astype(BF16)
+    def send_piece(at, n, rows):
+        ybuf[0, n, at] = rows.astype(BF16)
         for direction in range(2):
-            z_copy(q, n, direction).start()
+            z_copy(at, n, direction).start()
 
     def gather_near(n):
         for step in range(7):
             near_copy(n, step).wait_recv()
         low = nrec[n, :, :, :384].reshape(128, 384)
         high = nrec[n, :, :, 384:].reshape(128, 384)
-        send_piece(0, n, dot(compact(0, 0, 16), low) + dot(compact(0, 1, 16), high))
-
-    def gather_stage(q):
+        send_piece(0, n, dot(near_lines[0], low) + dot(near_lines[1], high))
+
+    def gather_stage(at):
+        q = X_ORDER[at]
         for step in range(7):
             block_copy(q, step).wait_recv()
-        low = rbuf[q - 1, :, :, :384].reshape(256, 384)
-        high = rbuf[q - 1, :, :, 384:].reshape(256, 384)
-        for n in range(3):
-            send_piece(q, n, dot(compact(n, 0, 32), low) + dot(compact(n, 1, 32), high))
-
-    def forward_stage(q, n):
-        z_copy(q, n, forward_direction(q, n)).wait_recv()
-        forward_copy(q, n).start()
-
-    def wait_rest(slot, q, n):
-        if slot == 2:
-            forward_copy(q, n).wait_recv()
-        elif slot != 0:
-            direction = 0 if slot == 3 else 1
-            if forward_direction(q, n) != direction:
-                z_copy(q, n, direction).wait_recv()
+
+        def piece(n):
+            low = rbuf[q - 1, :, :, :384].reshape(256, 384)
+            high = rbuf[q - 1, :, :, 384:].reshape(256, 384)
+            send_piece(at, n, dot(lines_of[n, 0], low) + dot(lines_of[n, 1], high))
+
+        loop(3, piece)
+
+    def forward_stage(at):
+        def piece(n):
+            z_copy(at, n, lax.rem(at + n, 2)).wait_recv()
+            forward_copy(at, n).start()
+
+        loop(3, piece)
+
+    def wait_other(at, n):
+        z_copy(at, n, lax.rem(at + n + 1, 2)).wait_recv()
 
     def find_places():
         ids = []
@@ -277,38 +280,55 @@
     def find_order(slot):
         c_at = lax.rem(c + slot, 4)
         lines = [[], []]
-        for q in X_ORDER:
+        for at, q in enumerate(X_ORDER):
             low = pl.multiple_of(c_at * 32 + lax.rem(x + q, 4) * 8, 8)
             one = places[pl.ds(low, 8), :]
             half = [jnp.broadcast_to(one[:, n:n + 1], (8, 128)) for n in range(9)]
-            if q == X_ORDER[3]:
-                lines = [line + [none, none] for line in lines]
+            if at == 2:
+                lines = [line + 12 * [none] for line in lines]
             lines[0] += half + [none]
             lines[1] += [none] + half
         for h in range(2):
-            wanted = jnp.transpose(jnp.concatenate(lines[h] + 6 * [none], axis=0))[0:1]
-            hit = jnp.where(iota((SLOTS, 384), 0).astype(F32) == wanted, scale, 0.0)
+            wanted = jnp.transpose(jnp.concatenate(lines[h] + 12 * [none], axis=0))[0:1]
+            hit = jnp.where(iota((SLOTS, 512), 0).astype(F32) == wanted, scale, 0.0)
             pmat[slot, h] = hit.astype(BF16)
 
-    def place_blocks(slot, n, side):
-        at = DENSE_ORDER.index(slot) * 32
+    def place_blocks(slot, n, side, out, at, add=False):
         for h in range(2):
-            if side == 0:
-                blocks = [ybuf[slot, n, i, h * 64:h * 64 + 80, :] for i in range(3)]
-                rows = dot(pmat[slot, h, :, :240], jnp.concatenate(blocks, axis=0))
-            else:
-                rows = dot(pmat[slot, h, :, 256:336], ybuf[slot, n, 3, h * 64:h * 64 + 80, :])
-            rows = rows.reshape(9, 32, 384)
+            blocks = [ybuf[slot, n, 2 * side + i, h * 64:h * 64 + 80, :] for i in range(2)]
+            order = pmat[slot, h, :, side * 256:side * 256 + 160]
+            rows = dot(order, jnp.concatenate(blocks, axis=0)).reshape(9, 32, 384)
             cols = slice(h * 384, (h + 1) * 384)
-            if side == 1:
-                rows = rows + dense[n, :, at:at + 32, cols].astype(F32)
-            dense[n, :, at:at + 32, cols] = rows.astype(BF16)
-
-    def multiply(total, n, low, high):
-        def add(t, total):
-            return total + dot(dense[n, t, low:high, :], v[n, t].reshape(SLAB, 512))
-
-        return lax.fori_loop(0, 9, add, total)
+            if add:
+                rows = rows + out[:, at, :, cols].astype(F32)
+            out[:, at, :, cols] = rows.astype(BF16)
+
+    def multiply(n, blocks, rows):
+        def add(i):
+            for half in range(2):
+                cols = slice(half * 256, half * 256 + 256)
+                some = [
+                    dot(blocks[3 * i + t].reshape(rows, SLAB), v[n, 3 * i + t, :, :, :, cols].reshape(SLAB, 256))
+                    for t in range(3)
+                ]
+                total[128 - rows:, cols] += some[0] + some[1] + some[2]
+
+        loop(3, add)
+
+    def multiply_early(n):
+        for b in range(3):
+            load_v(n, b).wait()
+        multiply(n, dense.at[n], 128)
+
+    def multiply_late(n):
+        wait_other(2, n)
+        wait_other(3, n)
+        loop(2, lambda i: place_blocks(1 + 2 * i, n, 1, late, 2 * i))
+        forward_copy(2, n).wait_recv()
+        forward_copy(3, n).wait_recv()
+        place_blocks(2, n, 1, late, 1)
+
+        multiply(n, late, 96)
 
     def sum_copy(slot, step):
         c_at = lax.rem(c + slot, 4)
@@ -322,77 +342,78 @@
             device_id_type=MESH,
         )
 
-    def send_sums(slot, total):
-        cbuf[lax.rem(c + slot, 4)] = total.reshape(4, 8, 512)
+    def send_sums(slot):
+        cbuf[lax.rem(c + slot, 4)] = total[slot * 32:(slot + 1) * 32].reshape(4, 8, 512)
         for step in range(1, 4):
             sum_copy(slot, step).start()
 
-    sort_stage(0)
+    sort_stage(0, True)
     for n in range(3):
         for b in range(3):
             load_v(n, b).start()
-    sort_stage(1)
-    sort_stage(3)
+
+    near_lines[0] = compact(0, 0, 16)
+    near_lines[1] = compact(0, 1, 16)
     for n in range(3):
-        gather_near(n)
+        for h in range(2):
+            lines_of[n, h] = compact(n, h, 32)
+
+    def far_stage(i):
+        q = 1 + 2 * i - 3 * (i // 2)
+
+        @pl.when(i == 2)
+        def _():
+            loop(3, gather_near)
+
+        sort_stage(q, False)
+
+        @pl.when(i < 2)
+        def _():
+            x_copy(q).start()
+            for step in range(7):
+                near_copy(i, step).wait_send()
+            send_near(i + 1)
+
+    loop(3, far_stage)
     find_places()
     pass_blocks(1)
-    sort_stage(2)
-    for n in range(3):
-        forward_stage(0, n)
-    find_order(0)
+    x_copy(2).start()
+    loop(4, find_order)
+    forward_stage(0)
     pass_blocks(3)
     gather_stage(1)
-    for slot in (3, 1, 2):
-        find_order(slot)
+    gather_stage(2)
+    pass_blocks(2)
+    forward_stage(1)
+    loop(3, lambda n: place_blocks(0, n, 0, dense.at[n], 0))
     gather_stage(3)
+    loop(3, lambda n: place_blocks(0, n, 1, dense.at[n], 0, add=True))
     for n in range(3):
-        forward_stage(1, n)
-    pass_blocks(2)
+        wait_other(0, n)
+        wait_other(1, n)
+    loop(6, lambda i: place_blocks(1 + 2 * (i // 3), lax.rem(i, 3), 0, dense.at[lax.rem(i, 3)], 1 + 2 * (i // 3)))
+    total[...] = jnp.zeros((128, 512), F32)
+    forward_stage(2)
     for n in range(3):
-        place_blocks(0, n, 0)
-    gather_stage(2)
-    for n in range(3):
-        forward_stage(3, n)
-    for n in range(3):
-        for slot in (3, 1):
-            for q in X_ORDER[:3]:
-                wait_rest(slot, q, n)
-            place_blocks(slot, n, 0)
-        place_blocks(0, n, 1)
-    for n in range(3):
-        forward_stage(2, n)
-    for n in range(3):
-        for slot in (3, 1):
-            wait_rest(slot, 2, n)
-            place_blocks(slot, n, 1)
-    total = jnp.zeros((96, 512), F32)
-    for n in range(3):
-        for b in range(3):
-            load_v(n, b).wait()
-        total = multiply(total, n, 0, 96)
-    for at, slot in enumerate(DENSE_ORDER[:3]):
-        send_sums(slot, total[at * 32:(at + 1) * 32])
-    for n in range(3):
-        for q in X_ORDER[:3]:
-            wait_rest(2, q, n)
-        place_blocks(2, n, 0)
-    total = jnp.zeros((32, 512), F32)
-    for n in range(3):
-        wait_rest(2, 2, n)
-        place_blocks(2, n, 1)
-        total = multiply(total, n, 96, 128)
-    send_sums(2, total)
+        forward_copy(0, n).wait_recv()
+        forward_copy(1, n).wait_recv()
+    loop(3, lambda n: place_blocks(2, n, 0, dense.at[n], 2))
+    loop(3, multiply_early)
+    send_sums(0)
+    forward_stage(3)
+    loop(3, multiply_late)
+    for slot in range(1, 4):
+        send_sums(slot)
 
     for slot in range(4):
         for step in range(1, 4):
             sum_copy(slot, step).wait_recv()
     for c_at in range(4):
-        total = cbuf[c_at, e]
+        rows = cbuf[c_at, e]
         for step in range(1, 4):
-            total = total + yrec[step - 1, c_at]
+            rows = rows + yrec[step - 1, c_at]
         for n in range(4):
-            mixed[n, pl.ds(c_at, 8, stride=4), :] = total[:, n * 128:(n + 1) * 128]
+            mixed[n, pl.ds(c_at, 8, stride=4), :] = rows[:, n * 128:(n + 1) * 128]
     for n in range(4):
         out_ref[:, n * 128:(n + 1) * 128] = mixed[n]
 
@@ -402,9 +423,8 @@
             for step in range(7):
                 block_copy(q, step).wait_send()
         else:
-            for n in range(3):
-                for step in range(7):
-                    near_copy(n, step).wait_send()
+            for step in range(7):
+                near_copy(2, step).wait_send()
         for n in range(3):
             z_copy(q, n, 0).wait_send()
             z_copy(q, n, 1).wait_send()
@@ -433,8 +453,12 @@
             pltpu.VMEM((3, 8, 32, SLAB), BF16),
             pltpu.VMEM((3, 8, 32, SLAB), BF16),
             pltpu.VMEM((4, 3, 4, 144, 384), BF16),
-            pltpu.VMEM((4, 2, SLOTS, 384), BF16),
-            pltpu.VMEM((3, 9, 128, SLAB), BF16),
+            pltpu.VMEM((4, 2, SLOTS, 512), BF16),
+            pltpu.VMEM((3, 9, 4, 32, SLAB), BF16),
+            pltpu.VMEM((9, 3, 32, SLAB), BF16),
+            pltpu.VMEM((128, 512), F32),
+            pltpu.VMEM((2, 144, 128), BF16),
+            pltpu.VMEM((3, 2, 144, 256), BF16),
             pltpu.VMEM((128, 128), F32),
             pltpu.VMEM((128, 128), F32),
             pltpu.VMEM((4, 4, 8, 512), F32),

time: 80.7 us -> 76.7 us (0.950)
  Pallas kernels: 78.1 us -> 74 us
    pallas_call x1, Pallas kernels: 78.1 us -> 74 us  [per_device(): pl.pallas_call(kernel, out_shape=jax.ShapeDtypeStruct((32, 512), F32), in...]
where the time goes in v3:
time: 76.7 us; the launch traced here: 75.5 us
  Pallas kernels  74 us (96%)
  local copies, waits for them, and re-layouts  1.47 us (2%)
    pallas_call x1, Pallas kernels, per_device(): pl.pallas_call(kernel, out_shape=jax.ShapeDtypeStruct((32, 512), F32), in...  74 us

profile of v3, /device:TPU:4, one launch (start us, length us, event | category | flops | bytes accessed | tf_op | source)
XLA Modules:
  0.0 75.5 jit_solution(22169825533875305)
XLA Ops:
  0.0 74.0 %shard_map.55 = f32[32,512]{1,0:T(8,128)} custom-call(bf16[288,2304]{1,0:T(8,128)(2,1)} %packed_hbm.1, s32[288,128]{1,0:T(8,128)} %bitcast.3, s32[288]{0:T(512)} %flip_ref.1, bf16[9,3,16,3,16,512]{5,4,3,2,1,0:T(8,128)(2,1)} %bitcast.2, bf16[768,768]{1,0:T(8,128)(2,1)} %constant.2.clone.part_hbm), custom_call_target="tpu_custom_call" | custom-call | tf_op jit(solution)/shard_map/pallas_call | solution.py:440
  74.0 1.5 %copy.7 = f32[32,512]{1,0:T(8,128)} copy(f32[32,512]{1,0:T(8,128)} %shard_map.55) | data formatting | bytes 131072

commit v4 on v3

--- a/solution.py
+++ b/solution.py
@@ -304,16 +304,13 @@
             out[:, at, :, cols] = rows.astype(BF16)
 
     def multiply(n, blocks, rows):
-        def add(i):
-            for half in range(2):
-                cols = slice(half * 256, half * 256 + 256)
-                some = [
-                    dot(blocks[3 * i + t].reshape(rows, SLAB), v[n, 3 * i + t, :, :, :, cols].reshape(SLAB, 256))
-                    for t in range(3)
-                ]
-                total[128 - rows:, cols] += some[0] + some[1] + some[2]
-
-        loop(3, add)
+        for half in range(2):
+            cols = slice(half * 256, half * 256 + 256)
+            some = [
+                dot(blocks[t].reshape(rows, SLAB), v[n, t, :, :, :, cols].reshape(SLAB, 256))
+                for t in range(9)
+            ]
+            total[128 - rows:, cols] += sum(some[1:], some[0])
 
     def multiply_early(n):
         for b in range(3):
@@ -323,7 +320,8 @@
     def multiply_late(n):
         wait_other(2, n)
         wait_other(3, n)
-        loop(2, lambda i: place_blocks(1 + 2 * i, n, 1, late, 2 * i))
+        place_blocks(1, n, 1, late, 0)
+        place_blocks(3, n, 1, late, 2)
         forward_copy(2, n).wait_recv()
         forward_copy(3, n).wait_recv()
         place_blocks(2, n, 1, late, 1)
@@ -386,14 +384,14 @@
     pass_blocks(2)
     forward_stage(1)
     loop(3, lambda n: place_blocks(0, n, 0, dense.at[n], 0))
-    gather_stage(3)
-    loop(3, lambda n: place_blocks(0, n, 1, dense.at[n], 0, add=True))
     for n in range(3):
         wait_other(0, n)
         wait_other(1, n)
     loop(6, lambda i: place_blocks(1 + 2 * (i // 3), lax.rem(i, 3), 0, dense.at[lax.rem(i, 3)], 1 + 2 * (i // 3)))
     total[...] = jnp.zeros((128, 512), F32)
     forward_stage(2)
+    gather_stage(3)
+    loop(3, lambda n: place_blocks(0, n, 1, dense.at[n], 0, add=True))
     for n in range(3):
         forward_copy(0, n).wait_recv()
         forward_copy(1, n).wait_recv()

time: 76.7 us -> 74.6 us (0.973)
  Pallas kernels: 74 us -> 72.1 us
    pallas_call x1, Pallas kernels: 74 us -> 72.1 us  [per_device(): pl.pallas_call(kernel, out_shape=jax.ShapeDtypeStruct((32, 512), F32), in...]
where the time goes in v4:
time: 74.6 us; the launch traced here: 73.6 us
  Pallas kernels  72.1 us (97%)
  local copies, waits for them, and re-layouts  1.47 us (2%)
    pallas_call x1, Pallas kernels, per_device(): pl.pallas_call(kernel, out_shape=jax.ShapeDtypeStruct((32, 512), F32), in...  72.1 us

profile of v4, /device:TPU:4, one launch (start us, length us, event | category | flops | bytes accessed | tf_op | source)
XLA Modules:
  0.0 73.6 jit_solution(14977225083227627548)
XLA Ops:
  0.0 72.1 %shard_map.55 = f32[32,512]{1,0:T(8,128)} custom-call(bf16[288,2304]{1,0:T(8,128)(2,1)} %packed_hbm.1, s32[288,128]{1,0:T(8,128)} %bitcast.3, s32[288]{0:T(512)} %flip_ref.1, bf16[9,3,16,3,16,512]{5,4,3,2,1,0:T(8,128)(2,1)} %bitcast.2, bf16[768,768]{1,0:T(8,128)(2,1)} %constant.2.clone.part_hbm), custom_call_target="tpu_custom_call" | custom-call | tf_op jit(solution)/shard_map/pallas_call | solution.py:438
  72.1 1.5 %copy.7 = f32[32,512]{1,0:T(8,128)} copy(f32[32,512]{1,0:T(8,128)} %shard_map.55) | data formatting | bytes 131072

commit v5 on v4

--- a/solution.py
+++ b/solution.py
@@ -395,11 +395,15 @@
     for n in range(3):
         forward_copy(0, n).wait_recv()
         forward_copy(1, n).wait_recv()
-    loop(3, lambda n: place_blocks(2, n, 0, dense.at[n], 2))
-    loop(3, multiply_early)
+    for n in range(3):
+        place_blocks(2, n, 0, dense.at[n], 2)
+    for n in range(3):
+        multiply_early(n)
+        z_copy(3, n, (3 + n) % 2).wait_recv()
+        forward_copy(3, n).start()
     send_sums(0)
-    forward_stage(3)
-    loop(3, multiply_late)
+    for n in range(3):
+        multiply_late(n)
     for slot in range(1, 4):
         send_sums(slot)
 

time: 74.6 us -> 74.3 us (level)
  no operation moved by 1% of the time
where the time goes in v5:
time: 74.3 us; the launch traced here: 73.6 us
  Pallas kernels  72.1 us (97%)
  local copies, waits for them, and re-layouts  1.47 us (2%)
    pallas_call x1, Pallas kernels, per_device(): pl.pallas_call(kernel, out_shape=jax.ShapeDtypeStruct((32, 512), F32), in...  72.1 us

profile of v5, /device:TPU:4, one launch (start us, length us, event | category | flops | bytes accessed | tf_op | source)
XLA Modules:
  0.0 73.6 jit_solution(6264942742147182697)
XLA Ops:
  0.0 72.1 %shard_map.55 = f32[32,512]{1,0:T(8,128)} custom-call(bf16[288,2304]{1,0:T(8,128)(2,1)} %packed_hbm.1, s32[288,128]{1,0:T(8,128)} %bitcast.3, s32[288]{0:T(512)} %flip_ref.1, bf16[9,3,16,3,16,512]{5,4,3,2,1,0:T(8,128)(2,1)} %bitcast.2, bf16[768,768]{1,0:T(8,128)(2,1)} %constant.2.clone.part_hbm), custom_call_target="tpu_custom_call" | custom-call | tf_op jit(solution)/shard_map/pallas_call | solution.py:442
  72.2 1.5 %copy.7 = f32[32,512]{1,0:T(8,128)} copy(f32[32,512]{1,0:T(8,128)} %shard_map.55) | data formatting | bytes 131072
